TPU v7x, 32 devices: a whole 2x2x4 slice. The times are simulated.
32 devices in a mesh: segment: 4 (over y, x), tensor: 4 (over z), dp: 2 (over core).
Axes of the slice: x: 2, y: 2, z: 4, core: 2. Of those that a mesh axis runs over, the one named last changes fastest.
Arguments:
- tokens: bfloat16 [2, 256, 8192], P('dp', 'tensor'), may hold values from -6 to 6
- cotangent: bfloat16 [2, 256, 8192], P('dp', 'tensor'), may hold values from -1.1953125 to 1.1953125
- sequence_job: int32 [2], P('dp'), may hold values from 0 to 31
- section_layer_list: int32 [4], replicated, may hold values from 0 to 1, as said below
- section_norm_gain: bfloat16 [4, 8192], P('segment'), may hold values from 0.099609375 to 1.8984375
- query_matrix: bfloat16 [4, 8192, 4096], P('segment', None, 'tensor'), may hold values from -0.0625 to 0.0625
- key_matrix: bfloat16 [4, 8192, 512], P('segment', None, 'tensor'), may hold values from -0.0625 to 0.0625
- value_matrix: bfloat16 [4, 8192, 512], P('segment', None, 'tensor'), may hold values from -0.0625 to 0.0625
- output_matrix: bfloat16 [4, 4096, 8192], P('segment', 'tensor'), may hold values from -0.09375 to 0.09375
- adapter_down_all: bfloat16 [4, 8192, 512], P('segment', 'tensor'), may hold values from -0.0625 to 0.0625
- adapter_up_all: bfloat16 [4, 512, 4096], P('segment', None, 'tensor'), may hold values from -0.09375 to 0.09375
Outputs:
- grad_down: float32 [4, 8192, 512], P('segment', 'tensor')
- grad_up: float32 [4, 512, 4096], P('segment', None, 'tensor')
Inputs may be any that keep to these rules, and one draw needn't show every extreme that they name: `section_layer_list`: at least one section applies no layer and at least one applies one; each of the others applies none or one.
All inputs are finite; a program needn't handle non-finite values.
Results may differ from a plain program's by a relative error of at most 0.035.
Values may be sent and summed in bfloat16 or wider, within the bound.
No kernel may reach another device: no remote copies, remote signals or barrier semaphores. Data moves between devices by JAX's collectives and lax.ppermute only.
A program may use at most 192 MiB of HBM per device.

v0:
```python
import math

import jax
import jax.numpy as jnp
from jax import lax
from jax.sharding import PartitionSpec as P

HEAD_SIZE = 128
ADAPTER_RANK = 16
ADAPTER_JOBS = 32


ADAPTER_SCALE = 2.0
EPSILON = 1e-05


def as_sent(x):

    def short(part):
        return part.astype(jnp.bfloat16) if part.dtype == jnp.float32 else part

    return jax.tree.map(short, x)


def swapped(block, axis, bit):
    count = lax.axis_size(axis)
    route = []
    for low in range(count):
        high = low | 1 << bit
        if high != low and high < count:
            route += [(low, high), (high, low)]
    return lax.ppermute(block, axis, route)


def shifted(block, axis, distance):
    devices = range(lax.axis_size(axis))
    route = [(i - distance, i) for i in devices if i - distance in devices]
    return lax.ppermute(block, axis, route)


def rotate(inputs, head_count):
    sequence_count, row_count, width_all = inputs.shape
    head_dim = width_all // head_count
    half_dim = head_dim // 2
    shaped = inputs.reshape(sequence_count, row_count, head_count, head_dim)
    positions = jnp.arange(row_count, dtype=jnp.float32)
    exponent = jnp.arange(half_dim, dtype=jnp.float32) * (2.0 / head_dim)
    frequency = jnp.exp(-math.log(10000.0) * exponent)
    angles = positions[:, None] * frequency[None, :]
    cosine_table = jnp.cos(angles)[None, :, None, :]
    sine_table = jnp.sin(angles)[None, :, None, :]
    first_half = shaped[..., :half_dim]
    second_half = shaped[..., half_dim:]
    turned = jnp.concatenate(
        [
            first_half * cosine_table - second_half * sine_table,
            second_half * cosine_table + first_half * sine_table,
        ],
        axis=-1,
    )
    return turned.reshape(sequence_count, row_count, width_all)


def attend(query_rows, key_rows, value_rows, head_dim):
    sequence_count, row_count, query_span_width = query_rows.shape
    head_count = query_span_width // head_dim
    key_heads = key_rows.shape[-1] // head_dim
    group_size = head_count // key_heads
    rotated_queries = rotate(query_rows, head_count).reshape(
        sequence_count, row_count, key_heads, group_size, head_dim
    )
    rotated_keys = rotate(key_rows, key_heads).reshape(
        sequence_count, row_count, key_heads, head_dim
    )
    value_heads = value_rows.reshape(sequence_count, row_count, key_heads, head_dim)
    scores = jnp.einsum("bqhgd,bshd->bhgqs", rotated_queries, rotated_keys) / math.sqrt(head_dim)
    causal = jnp.arange(row_count)[:, None] >= jnp.arange(row_count)[None, :]
    scores = jnp.where(causal, scores, -1e30)
    weights = jnp.exp(scores)
    probability = weights / jnp.sum(weights, axis=-1, keepdims=True)
    output = jnp.einsum("bhgqs,bshd->bqhgd", probability, value_heads)
    return output.reshape(sequence_count, row_count, query_span_width)


def shards(
    tokens,
    cotangent,
    sequence_job,
    section_layer_list,
    section_norm_gain,
    query_matrix,
    key_matrix,
    value_matrix,
    output_matrix,
    adapter_down_all,
    adapter_up_all,
):
    segments = lax.axis_size("segment")
    segment_index = lax.axis_index("segment")
    tensor_index = lax.axis_index("tensor")
    gain_row = section_norm_gain[0].astype(jnp.float32)
    query_weight = query_matrix[0]
    key_weight = key_matrix[0]
    value_weight = value_matrix[0]
    out_weight = output_matrix[0]
    down_adapter = adapter_down_all[0]
    up_adapter = adapter_up_all[0]
    piece_width = down_adapter.shape[0]
    first_column = tensor_index * piece_width
    local_rows = tokens.shape[1]
    key_local = key_weight.shape[1]
    piece_count = HEAD_SIZE // key_local if key_local < HEAD_SIZE else 1
    bit_count = piece_count.bit_length() - 1
    layer_count = jnp.sum(jnp.where(jnp.arange(segments) == segment_index, section_layer_list, 0))
    applies = layer_count > 0
    onehot = (sequence_job[:, None] == jnp.arange(ADAPTER_JOBS, dtype=jnp.int32)[None, :]).astype(
        jnp.float32
    )
    picked_down = jnp.transpose(
        jnp.take(
            down_adapter.reshape(piece_width, ADAPTER_JOBS, ADAPTER_RANK), sequence_job, axis=1
        ),
        (1, 0, 2),
    )
    picked_up = jnp.take(
        up_adapter.reshape(ADAPTER_JOBS, ADAPTER_RANK, up_adapter.shape[1]), sequence_job, axis=0
    ).astype(jnp.float32)

    def gather_rows(sharded):
        return lax.all_gather(sharded, "tensor", axis=1, tiled=True)

    def scatter_rows(term_maker):
        return jnp.transpose(
            lax.psum_scatter(
                term_maker(jnp.int32(0), lax.axis_size("tensor") * local_rows).astype(jnp.bfloat16),
                "tensor",
                scatter_dimension=0,
                tiled=True,
            ).astype(jnp.float32),
            (1, 0, 2),
        )

    def reduced_sum(partial_addend):
        return lax.psum(partial_addend, "tensor")

    def trade(first_part, second_part, bit_number):
        return (
            swapped(as_sent(first_part), "tensor", bit_number).astype(first_part.dtype),
            swapped(as_sent(second_part), "tensor", bit_number).astype(second_part.dtype),
        )

    def segment_move(moving, offset):
        return shifted(moving, "segment", offset)

    def lower_side(bit_number):
        return tensor_index // 2**bit_number % 2 == 0

    def split_back(key_gradient, value_gradient):
        for bit_number in reversed(range(bit_count)):
            half_width = key_gradient.shape[-1] // 2
            low_here = lower_side(bit_number)
            mine_keys = jnp.where(
                low_here, key_gradient[..., :half_width], key_gradient[..., half_width:]
            )
            send_keys = jnp.where(
                low_here, key_gradient[..., half_width:], key_gradient[..., :half_width]
            )
            mine_values = jnp.where(
                low_here, value_gradient[..., :half_width], value_gradient[..., half_width:]
            )
            send_values = jnp.where(
                low_here, value_gradient[..., half_width:], value_gradient[..., :half_width]
            )
            got_keys, got_values = trade(send_keys, send_values, bit_number)
            key_gradient = mine_keys + got_keys
            value_gradient = mine_values + got_values
        return (key_gradient, value_gradient)

    def choose_rows(array, first_row, row_extent):
        return lax.dynamic_slice_in_dim(array, first_row, row_extent, 1)

    def out_term(attended, first_row, row_extent, layout_form):
        picked = choose_rows(attended, first_row, row_extent)
        return jnp.einsum(
            "brc,cd->" + layout_form, picked, out_weight, preferred_element_type=jnp.float32
        )

    def input_term(gradient_list, first_row, row_extent, layout_form):
        query_gradient, key_gradient, value_gradient, adapter_reverse = gradient_list
        partial_addend = jnp.einsum(
            "brc,dc->" + layout_form,
            choose_rows(query_gradient, first_row, row_extent),
            query_weight,
            preferred_element_type=jnp.float32,
        )
        partial_addend = partial_addend + jnp.einsum(
            "brc,dc->" + layout_form,
            choose_rows(key_gradient, first_row, row_extent),
            key_weight,
            preferred_element_type=jnp.float32,
        )
        partial_addend = partial_addend + jnp.einsum(
            "brc,dc->" + layout_form,
            choose_rows(value_gradient, first_row, row_extent),
            value_weight,
            preferred_element_type=jnp.float32,
        )
        adapter_piece = choose_rows(adapter_reverse, first_row, row_extent)
        adapter_piece = jnp.transpose(adapter_piece, (1, 0, 2))
        column_position = (
            lax.dynamic_slice_in_dim(partial_addend, first_column, piece_width, 2) + adapter_piece
        )
        return lax.dynamic_update_slice_in_dim(partial_addend, column_position, first_column, 2)

    def backward_core(grad_full, saved_layer):
        stream, inverse, normed_full, query_rows, key_rows, value_rows, reduced_rank = saved_layer
        grad_attended = jnp.einsum(
            "brd,cd->brc", grad_full, out_weight, preferred_element_type=jnp.float32
        )
        unused, pullback = jax.vjp(
            lambda first_in, second_in, third_in: attend(first_in, second_in, third_in, HEAD_SIZE),
            query_rows,
            key_rows,
            value_rows,
        )
        query_gradient, key_gradient, value_gradient = pullback(grad_attended)
        key_gradient, value_gradient = split_back(key_gradient, value_gradient)
        shared_up_adapter = ADAPTER_SCALE * jnp.einsum("mxh,mxi->mhi", reduced_rank, query_gradient)
        grad_up = jnp.einsum("bj,bkc->jkc", onehot, shared_up_adapter).reshape(
            ADAPTER_JOBS * ADAPTER_RANK, shared_up_adapter.shape[2]
        )
        reduced_gradient = reduced_sum(
            ADAPTER_SCALE * jnp.einsum("ehy,ety->eht", query_gradient, picked_up)
        )
        sliced = lax.dynamic_slice_in_dim(normed_full, first_column, piece_width, 2).astype(
            jnp.float32
        )
        share_down = jnp.einsum("brd,brk->bdk", sliced, reduced_gradient)
        grad_down = jnp.einsum("bj,bdk->djk", onehot, share_down).reshape(
            piece_width, ADAPTER_JOBS * ADAPTER_RANK
        )
        adapter_reverse = jnp.einsum(
            "aen,acn->aec", reduced_gradient, picked_down.astype(jnp.float32)
        )
        gradient_list = (
            query_gradient.astype(jnp.bfloat16),
            key_gradient.astype(jnp.bfloat16),
            value_gradient.astype(jnp.bfloat16),
            adapter_reverse,
        )
        return (gradient_list, grad_down, grad_up)

    carried = tokens
    saved_state = None
    for step_index in range(segments):
        normalize_stream = carried.astype(jnp.float32)
        normalize_inverse = lax.rsqrt(
            jnp.mean(normalize_stream * normalize_stream, axis=-1, keepdims=True) + EPSILON
        )
        normed = (normalize_stream * normalize_inverse * gain_row).astype(jnp.bfloat16)
        forward_normed_full = gather_rows(normed)
        projections_query_rows = jnp.einsum(
            "brd,dc->brc", forward_normed_full, query_weight, preferred_element_type=jnp.float32
        )
        projections_key_rows = jnp.einsum(
            "brd,dc->brc", forward_normed_full, key_weight, preferred_element_type=jnp.float32
        )
        projections_value_rows = jnp.einsum(
            "brd,dc->brc", forward_normed_full, value_weight, preferred_element_type=jnp.float32
        )
        projections_sliced = lax.dynamic_slice_in_dim(
            forward_normed_full, first_column, piece_width, 2
        )
        projections_reduced_rank = reduced_sum(
            jnp.einsum(
                "brd,bdk->brk", projections_sliced, picked_down, preferred_element_type=jnp.float32
            )
        )
        projections_query_rows = projections_query_rows + ADAPTER_SCALE * jnp.einsum(
            "aqw,awy->aqy", projections_reduced_rank, picked_up
        )
        pair_key_rows = projections_key_rows
        pair_value_rows = projections_value_rows
        for pair_bit_number in range(bit_count):
            other_keys, other_values = trade(pair_key_rows, pair_value_rows, pair_bit_number)
            pair_low_here = lower_side(pair_bit_number)
            pair_key_rows = jnp.where(
                pair_low_here,
                jnp.concatenate([pair_key_rows, other_keys], axis=-1),
                jnp.concatenate([other_keys, pair_key_rows], axis=-1),
            )
            pair_value_rows = jnp.where(
                pair_low_here,
                jnp.concatenate([pair_value_rows, other_values], axis=-1),
                jnp.concatenate([other_values, pair_value_rows], axis=-1),
            )
        projections_key_rows = pair_key_rows
        projections_value_rows = pair_value_rows
        forward_attended = attend(
            projections_query_rows, projections_key_rows, projections_value_rows, HEAD_SIZE
        ).astype(jnp.bfloat16)
        summed = scatter_rows(
            lambda first_row, row_extent: out_term(forward_attended, first_row, row_extent, "rbd")
        )
        updated = (normalize_stream + summed).astype(jnp.bfloat16)
        saved_now = (
            normalize_stream,
            normalize_inverse,
            forward_normed_full,
            projections_query_rows,
            projections_key_rows,
            projections_value_rows,
            projections_reduced_rank,
        )
        owner_here = segment_index == step_index
        if saved_state is None:
            saved_state = saved_now
        else:
            saved_state = jax.tree.map(
                lambda newer, older: jnp.where(owner_here, newer, older), saved_now, saved_state
            )
        result = jnp.where(applies, updated, carried)
        if step_index + 1 < segments:
            carried = segment_move(result, 1)
    gradient = cotangent.astype(jnp.float32)
    total_down = jnp.zeros((piece_width, ADAPTER_JOBS * ADAPTER_RANK), jnp.float32)
    total_up = jnp.zeros((ADAPTER_JOBS * ADAPTER_RANK, query_weight.shape[1]), jnp.float32)
    for step_index in range(segments):
        owner_segment = segments - 1 - step_index
        owner_here = (segment_index == owner_segment) & applies
        backward_grad_full = gather_rows(gradient.astype(jnp.bfloat16))
        backward_gradient_list, backward_grad_down, backward_grad_up = backward_core(
            backward_grad_full, saved_state
        )
        backward_grad_norm = scatter_rows(
            lambda first_row, row_extent: input_term(
                backward_gradient_list, first_row, row_extent, "rbd"
            )
        )
        norm_stream = saved_state[0]
        norm_inverse = saved_state[1]
        gained = backward_grad_norm * gain_row
        new_gradient = gradient + (
            norm_inverse * gained
            - norm_stream * norm_inverse**3 * jnp.mean(gained * norm_stream, axis=-1, keepdims=True)
        )
        grad_down = backward_grad_down
        grad_up = backward_grad_up
        total_down = jnp.where(owner_here, grad_down, total_down)
        total_up = jnp.where(owner_here, grad_up, total_up)
        result = jnp.where(applies, new_gradient, gradient)
        if step_index + 1 < segments:
            gradient = segment_move(result.astype(jnp.bfloat16), -1).astype(jnp.float32)
    total_down, total_up = (
        lax.psum(total_down.astype(jnp.bfloat16), "dp").astype(jnp.float32),
        lax.psum(total_up.astype(jnp.bfloat16), "dp").astype(jnp.float32),
    )
    return (total_down[None], total_up[None])


def solution(mesh):
    in_specs = (
        P("dp", "tensor", None),
        P("dp", "tensor", None),
        P("dp"),
        P(),
        P("segment", None),
        P("segment", None, "tensor"),
        P("segment", None, "tensor"),
        P("segment", None, "tensor"),
        P("segment", "tensor", None),
        P("segment", "tensor", None),
        P("segment", None, "tensor"),
    )
    out_specs = (P("segment", "tensor", None), P("segment", None, "tensor"))
    return jax.shard_map(shards, mesh=mesh, in_specs=in_specs, out_specs=out_specs, check_vma=False)
```

profile of v0, /device:TPU:0, one launch (start us, length us, event | category | flops | bytes accessed | tf_op | source)
XLA Modules:
  0.0 1751.5 jit_solution(18008607676478454491)
XLA Ops:
  17.4 78.4 %all-gather.9.cloned.1.call-done = bf16[1,256,8192]{2,1,0:T(8,128)(2,1)} async-done(((bf16[1,64,8192]{2,1,0:T(8,128)(2,1)}), bf16[1,256,8192]{2,1,0:T(8,128)(2,1)}) %all-gather.9.cloned.1.call-update) | async-done | bytes 4194320 | tf_op jit(solution)/shard_map/all_gather | solution.py:130
  102.2 16.0 psum.70
  145.8 73.3 %reduce-scatter.7.cloned.1.call-done = bf16[64,1,8192]{2,0,1:T(8,128)(2,1)} async-done(((bf16[256,1,8192]{2,0,1:T(8,128)(2,1)}), bf16[64,1,8192]{2,0,1:T(8,128)(2,1)}) %reduce-scatter.7.cloned.1.call-update) | async-done | bytes 1048592 | tf_op jit(solution)/shard_map/reduce_scatter | solution.py:134
  224.5 22.4 %collective-permute-done = bf16[1,64,8192]{2,1,0:T(8,128)(2,1)S(1)} collective-permute-done((bf16[1,64,8192]{2,1,0:T(8,128)(2,1)S(1)}, bf16[1,64,8192]{2,1,0:T(8,128)(2,1)S(1)}, u32[]{:S(2)}, u32[]{:S(2)}) %collective-permute-start) | collective-permute-done | bytes 1048608 | tf_op jit(solution)/shard_map/ppermute | solution.py:38
  249.2 82.4 %all-gather.11.cloned.1.call-done = bf16[1,256,8192]{2,1,0:T(8,128)(2,1)} async-done(((bf16[1,64,8192]{2,1,0:T(8,128)(2,1)}), bf16[1,256,8192]{2,1,0:T(8,128)(2,1)}) %all-gather.11.cloned.1.call-update) | async-done | bytes 4194320 | tf_op jit(solution)/shard_map/all_gather | solution.py:130
  333.2 16.0 psum.71
  375.0 75.3 %reduce-scatter.9.cloned.1.call-done = bf16[64,1,8192]{2,0,1:T(8,128)(2,1)} async-done(((bf16[256,1,8192]{2,0,1:T(8,128)(2,1)}), bf16[64,1,8192]{2,0,1:T(8,128)(2,1)}) %reduce-scatter.9.cloned.1.call-update) | async-done | bytes 1048592 | tf_op jit(solution)/shard_map/reduce_scatter | solution.py:134
  456.0 22.4 %collective-permute-done.1 = bf16[1,64,8192]{2,1,0:T(8,128)(2,1)S(1)} collective-permute-done((bf16[1,64,8192]{2,1,0:T(8,128)(2,1)S(1)}, bf16[1,64,8192]{2,1,0:T(8,128)(2,1)S(1)}, u32[]{:S(2)}, u32[]{:S(2)}) %collective-permute-start.1) | collective-permute-done | bytes 1048608 | tf_op jit(solution)/shard_map/ppermute | solution.py:38
  480.7 82.4 %all-gather.13.cloned.1.call-done = bf16[1,256,8192]{2,1,0:T(8,128)(2,1)} async-done(((bf16[1,64,8192]{2,1,0:T(8,128)(2,1)}), bf16[1,256,8192]{2,1,0:T(8,128)(2,1)}) %all-gather.13.cloned.1.call-update) | async-done | bytes 4194320 | tf_op jit(solution)/shard_map/all_gather | solution.py:130
  564.8 16.3 psum.72
  607.6 74.5 %reduce-scatter.11.cloned.1.call-done = bf16[64,1,8192]{2,0,1:T(8,128)(2,1)} async-done(((bf16[256,1,8192]{2,0,1:T(8,128)(2,1)}), bf16[64,1,8192]{2,0,1:T(8,128)(2,1)}) %reduce-scatter.11.cloned.1.call-update) | async-done | bytes 1048592 | tf_op jit(solution)/shard_map/reduce_scatter | solution.py:134
  689.7 21.8 %collective-permute-done.2 = bf16[1,64,8192]{2,1,0:T(8,128)(2,1)} collective-permute-done((bf16[1,64,8192]{2,1,0:T(8,128)(2,1)}, bf16[1,64,8192]{2,1,0:T(8,128)(2,1)}, u32[]{:S(2)}, u32[]{:S(2)}) %collective-permute-start.2) | collective-permute-done | bytes 1048608 | tf_op jit(solution)/shard_map/ppermute | solution.py:38
  716.2 48.8 %all-gather.17.cloned.1.call-done = bf16[1,256,8192]{2,1,0:T(8,128)(2,1)} async-done(((bf16[1,64,8192]{2,1,0:T(8,128)(2,1)}), bf16[1,256,8192]{2,1,0:T(8,128)(2,1)}) %all-gather.17.cloned.1.call-update) | async-done | bytes 4194320 | tf_op jit(solution)/shard_map/all_gather | solution.py:130
  775.1 71.5 %all-gather.15.cloned.1.call-done = bf16[1,256,8192]{2,1,0:T(8,128)(2,1)} async-done(((bf16[1,64,8192]{2,1,0:T(8,128)(2,1)}), bf16[1,256,8192]{2,1,0:T(8,128)(2,1)}) %all-gather.15.cloned.1.call-update) | async-done | bytes 4194320 | tf_op jit(solution)/shard_map/all_gather | solution.py:130
  852.8 16.5 psum.73
  900.5 16.1 psum.74
  916.6 13.9 fusion.10
  957.2 75.3 %reduce-scatter.13.cloned.1.call-done = bf16[64,1,8192]{2,0,1:T(8,128)(2,1)} async-done(((bf16[256,1,8192]{2,0,1:T(8,128)(2,1)}), bf16[64,1,8192]{2,0,1:T(8,128)(2,1)}) %reduce-scatter.13.cloned.1.call-update) | async-done | bytes 1048592 | tf_op jit(solution)/shard_map/reduce_scatter | solution.py:134
  1038.4 25.5 %collective-permute-done.3 = bf16[1,64,8192]{2,1,0:T(8,128)(2,1)S(1)} collective-permute-done((bf16[1,64,8192]{2,1,0:T(8,128)(2,1)S(1)}, bf16[1,64,8192]{2,1,0:T(8,128)(2,1)S(1)}, u32[]{:S(2)}, u32[]{:S(2)}) %collective-permute-start.3) | collective-permute-done | bytes 1048608 | tf_op jit(solution)/shard_map/ppermute | solution.py:38
  1065.2 81.2 %all-gather.19.cloned.1.call-done = bf16[1,256,8192]{2,1,0:T(8,128)(2,1)} async-done(((bf16[1,64,8192]{2,1,0:T(8,128)(2,1)}), bf16[1,256,8192]{2,1,0:T(8,128)(2,1)}) %all-gather.19.cloned.1.call-update) | async-done | bytes 4194320 | tf_op jit(solution)/shard_map/all_gather | solution.py:130
  1164.5 16.0 psum.75
  1180.5 13.9 fusion.8
  1221.1 75.2 %reduce-scatter.15.cloned.1.call-done = bf16[64,1,8192]{2,0,1:T(8,128)(2,1)} async-done(((bf16[256,1,8192]{2,0,1:T(8,128)(2,1)}), bf16[64,1,8192]{2,0,1:T(8,128)(2,1)}) %reduce-scatter.15.cloned.1.call-update) | async-done | bytes 1048592 | tf_op jit(solution)/shard_map/reduce_scatter | solution.py:134
  1302.1 25.5 %collective-permute-done.4 = bf16[1,64,8192]{2,1,0:T(8,128)(2,1)S(1)} collective-permute-done((bf16[1,64,8192]{2,1,0:T(8,128)(2,1)S(1)}, bf16[1,64,8192]{2,1,0:T(8,128)(2,1)S(1)}, u32[]{:S(2)}, u32[]{:S(2)}) %collective-permute-start.4) | collective-permute-done | bytes 1048608 | tf_op jit(solution)/shard_map/ppermute | solution.py:38
  1329.1 81.0 %all-gather.21.cloned.1.call-done = bf16[1,256,8192]{2,1,0:T(8,128)(2,1)} async-done(((bf16[1,64,8192]{2,1,0:T(8,128)(2,1)}), bf16[1,256,8192]{2,1,0:T(8,128)(2,1)}) %all-gather.21.cloned.1.call-update) | async-done | bytes 4194320 | tf_op jit(solution)/shard_map/all_gather | solution.py:130
  1428.2 16.3 psum.76
  1444.5 13.9 fusion.6
  1485.0 75.2 %reduce-scatter.17.cloned.1.call-done = bf16[64,1,8192]{2,0,1:T(8,128)(2,1)} async-done(((bf16[256,1,8192]{2,0,1:T(8,128)(2,1)}), bf16[64,1,8192]{2,0,1:T(8,128)(2,1)}) %reduce-scatter.17.cloned.1.call-update) | async-done | bytes 1048592 | tf_op jit(solution)/shard_map/reduce_scatter | solution.py:134
  1566.4 25.6 %collective-permute-done.5 = bf16[1,64,8192]{2,1,0:T(8,128)(2,1)} collective-permute-done((bf16[1,64,8192]{2,1,0:T(8,128)(2,1)S(1)}, bf16[1,64,8192]{2,1,0:T(8,128)(2,1)}, u32[]{:S(2)}, u32[]{:S(2)}) %collective-permute-start.5) | collective-permute-done | bytes 1048608 | tf_op jit(solution)/shard_map/ppermute | solution.py:38
  1601.2 72.4 %all-gather.23.cloned.1.call-done = bf16[1,256,8192]{2,1,0:T(8,128)(2,1)} async-done(((bf16[1,64,8192]{2,1,0:T(8,128)(2,1)}), bf16[1,256,8192]{2,1,0:T(8,128)(2,1)}) %all-gather.23.cloned.1.call-update) | async-done | bytes 4194320 | tf_op jit(solution)/shard_map/all_gather | solution.py:130
  1695.2 16.6 psum.77
  1717.2 21.8 %all-reduce.17.cloned.1.call-done = (bf16[1,2048,512]{1,2,0:T(8,128)(2,1)}, bf16[1,512,1024]{2,1,0:T(8,128)(2,1)}) async-done(((bf16[1,2048,512]{1,2,0:T(8,128)(2,1)}, bf16[1,512,1024]{2,1,0:T(8,128)(2,1)}), (bf16[1,2048,512]{1,2,0:T(8,128)(2,1)}, bf16[1,512,1024]{2,1,0:T(8,128)(2,1)})) %all-reduce.17.cloned.1.call-update) | async-done | bytes 3145744 | tf_op jit(solution)/shard_map/psum | solution.py:355
  (362 shorter events, 351.2 us)
Async XLA Ops:
  7.2 88.7 %copy-start = (bf16[1,8192,128]{2,1,0:T(8,128)(2,1)S(1)}, bf16[1,8192,128]{2,1,0:T(8,128)(2,1)}, u32[]{:S(2)}) copy-start(bf16[1,8192,128]{2,1,0:T(8,128)(2,1)} %param.17) | copy-start | bytes 6291460
  7.2 88.7 %all-gather.9.cloned.1.call-start = ((), (), s32[]{:S(2)}) async-start(), calls=%async_computation.6 | async-start | bytes 5242880 | tf_op jit(solution)/shard_map/all_gather | solution.py:130
  12.2 206.8 %reduce-scatter.7.cloned.1.call-start = ((), (), s32[]{:S(2)}) async-start(), calls=%async_computation.7 | async-start | bytes 5242880 | tf_op jit(solution)/shard_map/reduce_scatter | solution.py:134
  16.9 582.7 %copy-start.65 = (pred[256,256]{0,1:T(8,128)(4,1)}, pred[256,256]{0,1:T(8,128)(4,1)S(1)}, u32[]{:S(2)}) copy-start(pred[256,256]{0,1:T(8,128)(4,1)S(1)} %iota_compare_fusion) | copy-start | bytes 196612
  143.8 75.3 %copy-start.15 = (bf16[1,64,8192]{2,1,0:T(8,128)(2,1)S(1)}, bf16[1,64,8192]{2,1,0:T(8,128)(2,1)}, u32[]{:S(2)}) copy-start(bf16[1,64,8192]{2,1,0:T(8,128)(2,1)} %param.11) | copy-start | bytes 3145732
  143.8 187.9 %all-gather.11.cloned.1.call-start = ((), (), s32[]{:S(2)}) async-start(), calls=%async_computation.8 | async-start | bytes 5242880 | tf_op jit(solution)/shard_map/all_gather | solution.py:130
  220.6 26.3 %collective-permute-start = (bf16[1,64,8192]{2,1,0:T(8,128)(2,1)S(1)}, bf16[1,64,8192]{2,1,0:T(8,128)(2,1)S(1)}, u32[]{:S(2)}, u32[]{:S(2)}) collective-permute-start(bf16[1,64,8192]{2,1,0:T(8,128)(2,1)S(1)} %fusion.172), channel_id=1, source_target_pairs={{0,8},{8,16},{16,24},{1,9},{9,17},{17,25},{2,10},{10,18},{18,26},{... | collective-permute-start | bytes 3145736 | tf_op jit(solution)/shard_map/ppermute | solution.py:38
  249.2 201.1 %reduce-scatter.9.cloned.1.call-start = ((), (), s32[]{:S(2)}) async-start(), calls=%async_computation.9 | async-start | bytes 5242880 | tf_op jit(solution)/shard_map/reduce_scatter | solution.py:134
  375.0 188.2 %all-gather.13.cloned.1.call-start = ((), (), s32[]{:S(2)}) async-start(), calls=%async_computation.10 | async-start | bytes 5242880 | tf_op jit(solution)/shard_map/all_gather | solution.py:130
  452.5 25.8 %collective-permute-start.1 = (bf16[1,64,8192]{2,1,0:T(8,128)(2,1)S(1)}, bf16[1,64,8192]{2,1,0:T(8,128)(2,1)S(1)}, u32[]{:S(2)}, u32[]{:S(2)}) collective-permute-start(bf16[1,64,8192]{2,1,0:T(8,128)(2,1)S(1)} %fusion.171), channel_id=1, source_target_pairs={{0,8},{8,16},{16,24},{1,9},{9,17},{17,25},{2,10},{10,18},{18,26},{... | collective-permute-start | bytes 3145736 | tf_op jit(solution)/shard_map/ppermute | solution.py:38
  480.7 201.4 %reduce-scatter.11.cloned.1.call-start = ((), (), s32[]{:S(2)}) async-start(), calls=%async_computation.11 | async-start | bytes 5242880 | tf_op jit(solution)/shard_map/reduce_scatter | solution.py:134
  606.8 158.3 %all-gather.17.cloned.1.call-start = ((), (), s32[]{:S(2)}) async-start(), calls=%async_computation.13 | async-start | bytes 5242880 | tf_op jit(solution)/shard_map/all_gather | solution.py:130
  607.5 239.0 %all-gather.15.cloned.1.call-start = ((), (), s32[]{:S(2)}) async-start(), calls=%async_computation.12 | async-start | bytes 5242880 | tf_op jit(solution)/shard_map/all_gather | solution.py:130
  685.3 26.1 %collective-permute-start.2 = (bf16[1,64,8192]{2,1,0:T(8,128)(2,1)}, bf16[1,64,8192]{2,1,0:T(8,128)(2,1)}, u32[]{:S(2)}, u32[]{:S(2)}) collective-permute-start(bf16[1,64,8192]{2,1,0:T(8,128)(2,1)} %fusion.170), channel_id=1, source_target_pairs={{0,8},{8,16},{16,24},{1,9},{9,17},{17,25},{2,10},{10,18},{18,26},{... | collective-permute-start | bytes 3145736 | tf_op jit(solution)/shard_map/ppermute | solution.py:38
  713.6 585.1 %copy-start.69 = (f32[64]{0:T(128)}, f32[64]{0:T(128)S(1)}, u32[]{:S(2)}) copy-start(f32[64]{0:T(128)S(1)} %get-tuple-element.28) | copy-start | bytes 772
  716.1 316.4 %reduce-scatter.13.cloned.1.call-start = ((), (), s32[]{:S(2)}) async-start(), calls=%async_computation.14 | async-start | bytes 5242880 | tf_op jit(solution)/shard_map/reduce_scatter | solution.py:134
  957.2 78.6 %copy-start.71 = (f32[64]{0:T(128)S(1)}, f32[64]{0:T(128)}, u32[]{:S(2)}) copy-start(f32[64]{0:T(128)} %get-tuple-element.29) | copy-start | bytes 772
  957.2 189.2 %all-gather.19.cloned.1.call-start = ((), (), s32[]{:S(2)}) async-start(), calls=%async_computation.15 | async-start | bytes 5242880 | tf_op jit(solution)/shard_map/all_gather | solution.py:130
  1037.2 26.8 %collective-permute-start.3 = (bf16[1,64,8192]{2,1,0:T(8,128)(2,1)S(1)}, bf16[1,64,8192]{2,1,0:T(8,128)(2,1)S(1)}, u32[]{:S(2)}, u32[]{:S(2)}) collective-permute-start(bf16[1,64,8192]{2,1,0:T(8,128)(2,1)S(1)} %fusion.75), channel_id=1, source_target_pairs={{8,0},{16,8},{24,16},{9,1},{17,9},{25,17},{10,2},{18,10},{26,18},{... | collective-permute-start | bytes 3145736 | tf_op jit(solution)/shard_map/ppermute | solution.py:38
  1065.0 231.3 %reduce-scatter.15.cloned.1.call-start = ((), (), s32[]{:S(2)}) async-start(), calls=%async_computation.16 | async-start | bytes 5242880 | tf_op jit(solution)/shard_map/reduce_scatter | solution.py:134
  1160.3 34.1 %copy-start.19 = (bf16[1,256,8,128]{1,3,2,0:T(8,128)(2,1)}, bf16[1,256,8,128]{1,3,2,0:T(8,128)(2,1)S(1)}, u32[]{:S(2)}) copy-start(bf16[1,256,8,128]{1,3,2,0:T(8,128)(2,1)S(1)} %copy.101) | copy-start | bytes 1572868
  1221.0 77.7 %copy-start.26 = (bf16[1,64,8192]{2,1,0:T(8,128)(2,1)S(1)}, bf16[1,64,8192]{2,1,0:T(8,128)(2,1)}, u32[]{:S(2)}) copy-start(bf16[1,64,8192]{2,1,0:T(8,128)(2,1)} %copy-done.25) | copy-start | bytes 3145732
  1221.0 189.1 %all-gather.21.cloned.1.call-start = ((), (), s32[]{:S(2)}) async-start(), calls=%async_computation.17 | async-start | bytes 5242880 | tf_op jit(solution)/shard_map/all_gather | solution.py:130
  1300.8 26.8 %collective-permute-start.4 = (bf16[1,64,8192]{2,1,0:T(8,128)(2,1)S(1)}, bf16[1,64,8192]{2,1,0:T(8,128)(2,1)S(1)}, u32[]{:S(2)}, u32[]{:S(2)}) collective-permute-start(bf16[1,64,8192]{2,1,0:T(8,128)(2,1)S(1)} %fusion.76), channel_id=1, source_target_pairs={{8,0},{16,8},{24,16},{9,1},{17,9},{25,17},{10,2},{18,10},{26,18},{... | collective-permute-start | bytes 3145736 | tf_op jit(solution)/shard_map/ppermute | solution.py:38
  1328.7 231.6 %reduce-scatter.17.cloned.1.call-start = ((), (), s32[]{:S(2)}) async-start(), calls=%async_computation.18 | async-start | bytes 5242880 | tf_op jit(solution)/shard_map/reduce_scatter | solution.py:134
  1424.0 34.3 %copy-start.21 = (bf16[1,256,8,128]{1,3,2,0:T(8,128)(2,1)}, bf16[1,256,8,128]{1,3,2,0:T(8,128)(2,1)S(1)}, u32[]{:S(2)}) copy-start(bf16[1,256,8,128]{1,3,2,0:T(8,128)(2,1)S(1)} %copy.110) | copy-start | bytes 1572868
  1485.0 77.7 %copy-start.70 = (f32[64]{0:T(128)S(1)}, f32[64]{0:T(128)}, u32[]{:S(2)}) copy-start(f32[64]{0:T(128)} %copy-done.69) | copy-start | bytes 772
  1485.0 77.7 %copy-start.72 = (f32[64]{0:T(128)S(1)}, f32[64]{0:T(128)}, u32[]{:S(2)}) copy-start(f32[64]{0:T(128)} %get-tuple-element.29) | copy-start | bytes 772
  1485.0 188.5 %all-gather.23.cloned.1.call-start = ((), (), s32[]{:S(2)}) async-start(), calls=%async_computation.19 | async-start | bytes 5242880 | tf_op jit(solution)/shard_map/all_gather | solution.py:130
  1563.1 29.8 %copy-start.18 = (bf16[1,256,8,128]{1,3,2,0:T(8,128)(2,1)S(1)}, bf16[1,256,8,128]{1,3,2,0:T(8,128)(2,1)}, u32[]{:S(2)}) copy-start(bf16[1,256,8,128]{1,3,2,0:T(8,128)(2,1)} %copy.92) | copy-start | bytes 1572868
  1565.1 26.9 %collective-permute-start.5 = (bf16[1,64,8192]{2,1,0:T(8,128)(2,1)S(1)}, bf16[1,64,8192]{2,1,0:T(8,128)(2,1)}, u32[]{:S(2)}, u32[]{:S(2)}) collective-permute-start(bf16[1,64,8192]{2,1,0:T(8,128)(2,1)S(1)} %fusion.77), channel_id=1, source_target_pairs={{8,0},{16,8},{24,16},{9,1},{17,9},{25,17},{10,2},{18,10},{26,18},{... | collective-permute-start | bytes 3145736 | tf_op jit(solution)/shard_map/ppermute | solution.py:38
  1592.1 146.9 %all-reduce.17.cloned.1.call-start = ((), (), s32[]{:S(2)}) async-start(), calls=%async_computation.20 | async-start | bytes 6291456 | tf_op jit(solution)/shard_map/psum | solution.py:355
  (76 other events, 489.5 us)
Sparse Core Ops, SparseCore 0:
  12.4 83.4 all-gather.8
  143.9 75.1 reduce-scatter.6
  249.3 82.2 all-gather.10
  375.1 75.1 reduce-scatter.8
  480.8 82.2 all-gather.12
  606.9 75.1 reduce-scatter.10
  683.7 81.2 all-gather.16
  767.2 79.2 all-gather.14
  957.3 75.2 reduce-scatter.12
  1065.1 81.2 all-gather.18
  1221.1 75.1 reduce-scatter.14
  1328.8 81.2 all-gather.20
  1485.1 75.1 reduce-scatter.16
  1592.2 81.2 all-gather.22
  1717.3 21.6 all-reduce.16
where the time goes:
time: 1760 us; the launch traced here: 1750 us
  waiting for transfers between devices  1210 us (69%)
  matrix products  260 us (15%)
  blocking collectives  130 us (7%)
  other arithmetic  67.8 us (4%)
  local copies, waits for them, and re-layouts  47.4 us (3%)
    all_gather x8, waiting for transfers between devices, gather_rows(): return lax.all_gather(sharded, 'tensor', axis=1, tiled=True)  598 us
    reduce_scatter x6, waiting for transfers between devices, scatter_rows(): lax.psum_scatter(term_maker(jnp.int32(0), lax.axis_size('tensor') * local...  449 us
    ppermute x6, waiting for transfers between devices, shifted(): return lax.ppermute(block, axis, route)  143 us
    psum x8, blocking collectives, reduced_sum(): return lax.psum(partial_addend, 'tensor')  130 us
    dot_general x3, matrix products, input_term(): jnp.einsum('brc,dc->' + layout_form, choose_rows(query_gradient, first_ro...  41.7 us
    dot_general x4, matrix products, shards(): jnp.einsum('brd,dc->brc', forward_normed_full, query_weight, preferred_el...  38.4 us
    unnamed x183, local copies, waits for them, and re-layouts  37.5 us
  transfers between devices with their start and end apart: 21, of which 21 were waited for; matrix products, arithmetic and copies ran while one was open for 2% of the time, Pallas kernels for 0%

commit v1 on v0

v1 whole, which is shorter than its diff:
```python
import math

import jax
import jax.numpy as jnp
from jax import lax
from jax.sharding import PartitionSpec as P

HEAD_SIZE = 128
ADAPTER_RANK = 16
ADAPTER_JOBS = 32
ADAPTER_SCALE = 2.0
EPSILON = 1e-05

S, T, D = "segment", "tensor", "dp"
FEW = 4


def put(buffer, block, index):
    return lax.dynamic_update_slice_in_dim(buffer, block[None], index, 0)


def pick(stack, index):
    return lax.dynamic_index_in_dim(stack, index, 0, keepdims=False)


def rolled(block, columns, distance):
    nz = lax.axis_size(T)
    route = [(c * nz + z, c * nz + (z + distance) % nz) for c in columns for z in range(nz)]
    return lax.ppermute(block, (S, T), route)


def across(block, moves):
    nz = lax.axis_size(T)
    return lax.ppermute(block, (S, T), [(a * nz + z, b * nz + z) for a, b in moves for z in range(nz)])


def tensor_sum(stack, columns):
    nz, zi = lax.axis_size(T), lax.axis_index(T)
    total = pick(stack, zi).astype(jnp.float32)
    for r in range(1, nz):
        total = total + rolled(pick(stack, (zi + r) % nz), columns, r).astype(jnp.float32)
    return total.astype(stack.dtype)


def tensor_gather(block, columns):
    nz, zi = lax.axis_size(T), lax.axis_index(T)
    buffer = put(jnp.zeros((nz,) + block.shape, block.dtype), block, zi)
    for r in range(1, nz):
        buffer = put(buffer, rolled(block, columns, r), (zi - r) % nz)
    return buffer


def hop(partial, source, target):
    nz, me = lax.axis_size(T), lax.axis_index(S)
    rows, width = partial.shape
    groups = partial.reshape(nz, 4, rows // (4 * nz), width)
    to_x = across(groups[:, 2], [(source, source ^ 1)])
    to_y = across(groups[:, 3], [(source, source ^ 2)])
    own = tensor_sum(groups[:, 0:2], [source])
    one = tensor_sum(jnp.where(me == (source ^ 1), to_x, to_y), [source ^ 1, source ^ 2])
    if source ^ target == 3:
        by_x = across(jnp.where(me == source, own[1], one), [(source, target ^ 2), (target ^ 1, target)])
        by_y = across(jnp.where(me == source, own[0], one), [(source, target ^ 1), (target ^ 2, target)])
        pair = jnp.stack([by_y, by_x])
        single = jnp.where(me == (target ^ 2), by_x, by_y)
    else:
        rest = 3 - (source ^ target)
        got = across(jnp.where(me == source, own[1], one), [(source, target), (source ^ rest, target ^ rest)])
        pair = jnp.stack([got, one])
        single = jnp.where(me == source, own[0], got)
    gathered = tensor_gather(single, [target ^ 1, target ^ 2])
    from_x = across(gathered, [(target ^ 1, target)])
    from_y = across(gathered, [(target ^ 2, target)])
    two = tensor_gather(pair, [target])
    if source ^ target == 1:
        parts = [from_x, two[:, 0], two[:, 1], from_y]
    elif source ^ target == 2:
        parts = [from_y, two[:, 0], from_x, two[:, 1]]
    else:
        parts = [from_x, from_y, two[:, 0], two[:, 1]]
    return jnp.stack(parts, axis=1).reshape(rows, width)


def plain_hop(partial, source, target):
    shard = lax.psum_scatter(partial, T, scatter_dimension=0, tiled=True)
    shard = across(shard, [(source, target)])
    return lax.all_gather(shard, T, axis=0, tiled=True)


def spread(block):
    n, nz = lax.axis_size(S), lax.axis_size(T)
    me = lax.axis_index(S)
    rows, width = block.shape
    if n != 4 or width % 2048 or nz % 2 or nz > FEW:
        return lax.all_gather(block, T, axis=0, tiled=True)
    unit = width // 16 * 3
    first = width - 4 * unit
    mine = tensor_gather(lax.dynamic_slice_in_dim(block, first + me * unit, unit, 1), range(n))
    half = nz // 2
    x_swap = [(c, c ^ 1) for c in range(n)]
    y_swap = [(c, c ^ 2) for c in range(n)]
    by_x = across(mine, x_swap)
    by_y = across(mine, y_swap)
    far_low = across(by_y[:half], x_swap)
    far_high = across(by_x[half:], y_swap)
    block, unused = lax.optimization_barrier((block, mine))
    base = tensor_gather(block[:, :first], range(n))
    out = jnp.zeros((nz, rows, width), block.dtype)
    out = lax.dynamic_update_slice(out, base, (0, 0, 0))
    for piece, column, z in (
        (mine, me, 0),
        (by_x, me ^ 1, 0),
        (by_y, me ^ 2, 0),
        (far_low, me ^ 3, 0),
        (far_high, me ^ 3, half),
    ):
        out = lax.dynamic_update_slice(out, piece, (z, 0, first + column * unit))
    return out.reshape(nz * rows, width)


def swapped(block, bit):
    count = lax.axis_size(T)
    return lax.ppermute(block, T, [(i, i ^ 1 << bit) for i in range(count)])


def tensor_total(block):
    nz = lax.axis_size(T)
    if nz & (nz - 1):
        return lax.psum(block, T)
    for bit in range(nz.bit_length() - 1):
        block = block + swapped(block, bit)
    return block


def rotate(inputs, head_count):
    row_count, width_all = inputs.shape
    head_dim = width_all // head_count
    half_dim = head_dim // 2
    shaped = inputs.reshape(row_count, head_count, head_dim)
    positions = jnp.arange(row_count, dtype=jnp.float32)
    exponent = jnp.arange(half_dim, dtype=jnp.float32) * (2.0 / head_dim)
    frequency = jnp.exp(-math.log(10000.0) * exponent)
    angles = positions[:, None] * frequency[None, :]
    cosine_table = jnp.cos(angles)[:, None, :]
    sine_table = jnp.sin(angles)[:, None, :]
    first_half = shaped[..., :half_dim]
    second_half = shaped[..., half_dim:]
    turned = jnp.concatenate(
        [
            first_half * cosine_table - second_half * sine_table,
            second_half * cosine_table + first_half * sine_table,
        ],
        axis=-1,
    )
    return turned.reshape(row_count, width_all)


def attend(query_rows, key_rows, value_rows):
    row_count, query_width = query_rows.shape
    head_count = query_width // HEAD_SIZE
    key_heads = key_rows.shape[-1] // HEAD_SIZE
    rotated_queries = rotate(query_rows, head_count).reshape(row_count, key_heads, -1, HEAD_SIZE)
    rotated_keys = rotate(key_rows, key_heads).reshape(row_count, key_heads, HEAD_SIZE)
    value_heads = value_rows.reshape(row_count, key_heads, HEAD_SIZE)
    scores = jnp.einsum("qhgd,shd->hgqs", rotated_queries, rotated_keys) / math.sqrt(HEAD_SIZE)
    causal = jnp.arange(row_count)[:, None] >= jnp.arange(row_count)[None, :]
    scores = jnp.where(causal, scores, -1e30)
    weights = jnp.exp(scores)
    probability = weights / jnp.sum(weights, axis=-1, keepdims=True)
    output = jnp.einsum("hgqs,shd->qhgd", probability, value_heads)
    return output.reshape(row_count, query_width)


def dot(a, b, dims=((1,), (0,))):
    return lax.dot_general(a, b, (dims, ((), ())), preferred_element_type=jnp.float32)


def sequence_gradients(tokens, cotangent, job, sections, gain, weights, adapters):
    query_weight, key_weight, value_weight, out_weight = weights
    down_adapter, up_adapter = adapters
    n, nz = lax.axis_size(S), lax.axis_size(T)
    me, zi = lax.axis_index(S), lax.axis_index(T)
    local_rows, width = tokens.shape
    rows = local_rows * nz
    piece_width = down_adapter.shape[0]
    key_local = key_weight.shape[1]
    bits = (HEAD_SIZE // key_local).bit_length() - 1 if key_local < HEAD_SIZE else 0
    count, order, applies = sections

    picked_down = lax.dynamic_slice_in_dim(down_adapter, job * ADAPTER_RANK, ADAPTER_RANK, 1)
    if nz > FEW:
        picked_down = lax.all_gather(picked_down, T, axis=0, tiled=True)
    else:
        picked_down = tensor_gather(picked_down, range(n)).reshape(width, ADAPTER_RANK)
    picked_up = lax.dynamic_slice_in_dim(up_adapter, job * ADAPTER_RANK, ADAPTER_RANK, 0)
    here = (jnp.arange(rows) // local_rows == zi)[:, None]

    def low_side(bit):
        return zi // 2**bit % 2 == 0

    def share_heads(block):
        for bit in range(bits):
            other = swapped(block.astype(jnp.bfloat16), bit).astype(block.dtype)
            block = jnp.where(
                low_side(bit), jnp.concatenate([block, other], -1), jnp.concatenate([other, block], -1)
            )
        return block

    def split_back(block):
        for bit in reversed(range(bits)):
            half = block.shape[-1] // 2
            keep = jnp.where(low_side(bit), block[:, :half], block[:, half:])
            send = jnp.where(low_side(bit), block[:, half:], block[:, :half])
            block = keep + swapped(send.astype(jnp.bfloat16), bit).astype(block.dtype)
        return block

    def forward(hidden):
        stream = hidden.astype(jnp.float32)
        inverse = lax.rsqrt(jnp.mean(stream * stream, axis=-1, keepdims=True) + EPSILON)
        normed = (stream * inverse * gain).astype(jnp.bfloat16)
        low_rank = dot(normed, picked_down)
        queries = dot(normed, query_weight) + ADAPTER_SCALE * dot(low_rank, picked_up.astype(jnp.float32))
        key_own, value_own = dot(normed, key_weight), dot(normed, value_weight)
        keys, values = share_heads(key_own), share_heads(value_own)
        return hidden, inverse, normed, low_rank, queries, keys, values, key_own, value_own

    def project_out(state):
        attended = attend(state[4], state[5], state[6]).astype(jnp.bfloat16)
        return (dot(attended, out_weight) + jnp.where(here, state[0], 0).astype(jnp.float32)).astype(jnp.bfloat16)

    def backward(grad, state):
        queries, keys, values = state[4:7]
        grad_attended = dot(grad, out_weight, ((1,), (1,)))
        unused, pullback = jax.vjp(attend, queries, keys, values)
        grad_query, grad_keys, grad_values = pullback(grad_attended)
        grad_keys, grad_values = split_back(grad_keys), split_back(grad_values)
        grad_low = ADAPTER_SCALE * dot(grad_query, picked_up.astype(jnp.float32), ((1,), (1,)))
        return grad_query, grad_keys, grad_values, grad_low

    def project_in(grad, state, gradients):
        hidden, inverse, normed, low_rank, queries, keys, values, key_own, value_own = state
        grad_query, grad_keys, grad_values, grad_low = gradients
        back = (
            dot(grad_query.astype(jnp.bfloat16), query_weight, ((1,), (1,)))
            + dot(grad_keys.astype(jnp.bfloat16), key_weight, ((1,), (1,)))
            + dot(grad_values.astype(jnp.bfloat16), value_weight, ((1,), (1,)))
            + dot(grad_low, picked_down.astype(jnp.float32), ((1,), (1,)))
        )
        along = (
            jnp.sum(grad_query * queries, -1, keepdims=True)
            + jnp.sum(grad_keys * key_own, -1, keepdims=True)
            + jnp.sum(grad_values * value_own, -1, keepdims=True)
        ) / width
        stream = hidden.astype(jnp.float32)
        result = inverse * (back * gain) - stream * (inverse**2 * along)
        return (result + jnp.where(here, grad, 0).astype(jnp.float32)).astype(jnp.bfloat16)

    def travel(partial, start, end, ascending):
        pairs = [(a, b) for a in range(n) for b in range(n) if (a < b if ascending else a > b)]
        number = sum(jnp.where((start == a) & (end == b), i, 0) for i, (a, b) in enumerate(pairs))
        way = hop if n == 4 and nz <= FEW and local_rows % n == 0 else plain_hop
        return lax.switch(number, [lambda x, a=a, b=b: way(x, a, b) for a, b in pairs], partial)

    hidden = spread(tokens)

    def run(active):
        def branch(hidden):
            grad = spread(lax.optimization_barrier((cotangent, hidden))[0])
            state = forward(hidden)
            for j in range(1, active):
                got = travel(project_out(state), order[j - 1], order[j], True)
                state = forward(jnp.where(me == order[j], got, state[0]))
            gradients = backward(grad, state)
            for j in reversed(range(1, active)):
                got = travel(project_in(grad, state, gradients), order[j], order[j - 1], False)
                grad = jnp.where(me == order[j - 1], got, grad)
                gradients = backward(grad, state)
            grad_query, unused, unused, grad_low = gradients
            grad_up = ADAPTER_SCALE * dot(state[3], grad_query, ((0,), (0,)))
            grad_low = tensor_total(grad_low)
            mine = lax.dynamic_slice_in_dim(state[2], zi * piece_width, piece_width, 1)
            grad_down = dot(mine.astype(jnp.float32), grad_low, ((0,), (0,)))
            return grad_down, grad_up

        return branch

    grad_down, grad_up = lax.switch(count - 1, [run(active) for active in range(1, n)], hidden)
    return jnp.where(applies, grad_down, 0.0), jnp.where(applies, grad_up, 0.0)


def shards(
    tokens,
    cotangent,
    sequence_job,
    section_layer_list,
    section_norm_gain,
    query_matrix,
    key_matrix,
    value_matrix,
    output_matrix,
    adapter_down_all,
    adapter_up_all,
):
    n = lax.axis_size(S)
    gain = section_norm_gain[0].astype(jnp.float32)
    active = section_layer_list > 0
    rank = jnp.cumsum(active.astype(jnp.int32))
    order = [
        jnp.sum(jnp.where(active & (rank == j + 1), jnp.arange(n, dtype=jnp.int32), 0)) for j in range(n - 1)
    ]
    applies = jnp.sum(jnp.where(jnp.arange(n) == lax.axis_index(S), section_layer_list, 0)) > 0
    sections = (jnp.sum(active.astype(jnp.int32)), order, applies)
    weights = (query_matrix[0], key_matrix[0], value_matrix[0], output_matrix[0])
    adapters = (adapter_down_all[0], adapter_up_all[0])

    parts = [
        sequence_gradients(tokens[b], cotangent[b], sequence_job[b], sections, gain, weights, adapters)
        for b in range(tokens.shape[0])
    ]
    down = jnp.stack([p[0] for p in parts])
    up = jnp.stack([p[1] for p in parts])
    nd = lax.axis_size(D)
    downs, ups, jobs = [down], [up], [sequence_job]
    for r in range(1, nd):
        route = [(i, (i + r) % nd) for i in range(nd)]
        downs.append(lax.ppermute(down, D, route))
        ups.append(lax.ppermute(up, D, route))
        jobs.append(lax.ppermute(sequence_job, D, route))
    jobs = jnp.concatenate(jobs)
    wanted = (jobs[:, None] * ADAPTER_RANK + jnp.arange(ADAPTER_RANK, dtype=jnp.int32)[None, :]).reshape(-1, 1)
    place = (wanted == jnp.arange(ADAPTER_JOBS * ADAPTER_RANK, dtype=jnp.int32)[None, :]).astype(jnp.float32)
    downs = jnp.concatenate([x for block in downs for x in block], axis=1)
    ups = jnp.concatenate([x for block in ups for x in block], axis=0)
    grad_down = lax.dot_general(downs, place, (((1,), (0,)), ((), ())), precision=lax.Precision.HIGHEST)
    grad_up = lax.dot_general(place, ups, (((0,), (0,)), ((), ())), precision=lax.Precision.HIGHEST)
    return grad_down[None], grad_up[None]


def solution(mesh):
    in_specs = (
        P("dp", "tensor", None),
        P("dp", "tensor", None),
        P("dp"),
        P(),
        P("segment", None),
        P("segment", None, "tensor"),
        P("segment", None, "tensor"),
        P("segment", None, "tensor"),
        P("segment", "tensor", None),
        P("segment", "tensor", None),
        P("segment", None, "tensor"),
    )
    out_specs = (P("segment", "tensor", None), P("segment", None, "tensor"))
    return jax.shard_map(shards, mesh=mesh, in_specs=in_specs, out_specs=out_specs, check_vma=False)
```

time: 1760 us -> 624 us (0.35)
  waiting for transfers between devices: 1210 us -> 195 us
  starting transfers between devices: 17 us -> 150 us
  blocking collectives: 130 us -> 0 us
  matrix products: 260 us -> 138 us
  loops' own time: 0 us -> 45.1 us
  other arithmetic: 67.8 us -> 47.9 us
    all_gather x8 -> x0, waiting for transfers between devices: 598 us -> none  [gather_rows(): return lax.all_gather(sharded, 'tensor', axis=1, tiled=True)]
    reduce_scatter x6 -> x0, waiting for transfers between devices: 449 us -> none  [scatter_rows(): lax.psum_scatter(term_maker(jnp.int32(0), lax.axis_size('tensor') * local...]
    ppermute x6 -> x62, starting transfers between devices: 15.5 us -> 150 us  [the longest x39 101 us: rolled(): return lax.ppermute(block, (S, T), route)]
    dot_general x68 -> x28, matrix products: 260 us -> 129 us  [the longest x17 94.4 us: dot(): lax.dot_general(a, b, (dims, ((), ())), preferred_element_type=jnp.float32)]
    psum x8 -> x0, blocking collectives: 130 us -> none  [reduced_sum(): return lax.psum(partial_addend, 'tensor')]
    ppermute x6 -> x62, waiting for transfers between devices: 143 us -> 195 us  [the longest x39 106 us: rolled(): return lax.ppermute(block, (S, T), route)]
    another operation x0 -> x3, loops' own time: none -> 45.1 us  [the longest x1 31.7 us: sequence_gradients(): lax.switch(count - 1, [run(active) for active in range(1, n)], hidden)]
    unnamed x183 -> x18, local copies, waits for them, and re-layouts: 37.5 us -> 0.37 us
  transfers between devices with their start and end apart: 21 -> 62, of which waited for: 21 -> 27; matrix products, arithmetic and copies ran while one was open for 2% -> 11% of each run, Pallas kernels for 0% -> 0%
where the time goes in v1:
time: 624 us; the launch traced here: 625 us
  waiting for transfers between devices  195 us (31%)
  starting transfers between devices  150 us (24%)
  matrix products  138 us (22%)
  other arithmetic  47.9 us (8%)
  local copies, waits for them, and re-layouts  46.1 us (7%)
  loops' own time  45.1 us (7%)
    ppermute x39, waiting for transfers between devices, rolled(): return lax.ppermute(block, (S, T), route)  106 us
    ppermute x39, starting transfers between devices, rolled(): return lax.ppermute(block, (S, T), route)  101 us
    dot_general x17, matrix products, dot(): lax.dot_general(a, b, (dims, ((), ())), preferred_element_type=jnp.float32)  94.4 us
    ppermute x18, waiting for transfers between devices, across(): lax.ppermute(block, (S, T), [(a * nz + z, b * nz + z) for a, b in moves f...  83.8 us
    another operation x1, loops' own time, sequence_gradients(): lax.switch(count - 1, [run(active) for active in range(1, n)], hidden)  31.7 us
    ppermute x18, starting transfers between devices, across(): lax.ppermute(block, (S, T), [(a * nz + z, b * nz + z) for a, b in moves f...  28.5 us
    dot_general x4, matrix products, attend(): output = jnp.einsum('hgqs,shd->qhgd', probability, value_heads)  20.5 us
    another operation x2, loops' own time, travel(): lax.switch(number, [lambda x, a=a, b=b: way(x, a, b) for a, b in pairs],...  13.4 us
  transfers between devices with their start and end apart: 62, of which 27 were waited for; matrix products, arithmetic and copies ran while one was open for 11% of the time, Pallas kernels for 0%

profile of v1, /device:TPU:0, one launch (start us, length us, event | category | flops | bytes accessed | tf_op | source)
XLA Modules:
  0.0 625.0 jit_solution(6656311842574621890)
XLA Ops:
  14.0 5.8 collective-permute-start.670
  23.6 5.7 collective-permute-start.671
  30.8 5.7 collective-permute-start.672
  56.1 9.8 %collective-permute-done.664 = bf16[64,2048]{1,0:T(8,128)(2,1)S(1)} collective-permute-done((bf16[64,2048]{1,0:T(8,128)(2,1)S(1)}, bf16[64,2048]{1,0:T(8,128)(2,1)S(1)}, u32[]{:S(2)}, u32[]{:S(2)}) %collective-permute-start.664) | collective-permute-done | bytes 262176 | tf_op jit(solution)/shard_map/ppermute | solution.py:29
  75.6 6.0 collective-permute-done.668
  84.8 521.6 %conditional.7 = (f32[2048,16]{0,1:T(8,128)S(1)}, f32[16,1024]{1,0:T(8,128)}) conditional(s32[]{:T(128)} %clamp.21, (bf16[256,8192]{1,0:T(8,128)(2,1)}, f32[8192]{0:T(1024)S(1)}, s32[]{:T(128)}, bf16[64,8192]{1,0:T(8,128)(2,1)S(1)}, bf16[1024,8192]{1,0:T(8,128)(2,1)}, /*index=5*/bf16[8192,128]{1,0:T(8,128)(2,1)}, ...), branch_computations={%region_5.0_spmd, %region_9.31_spmd, %region_31.72_spmd} | conditional | flops 50953629696 | bytes 1193471488 | solution.py:287
  109.9 11.7 %fusion.357 = f32[32,8,8,128]{3,1,2,0:T(8,128)S(1)} fusion(f32[256,1024]{1,0:T(8,128)} %convolution_multiply_fusion.4, bf16[256,8192]{1,0:T(8,128)(2,1)} %fusion.328, bf16[8192,1024]{1,0:T(8,128)(2,1)} %get-tuple-element.188), kind=kOutput, calls=%fused_computation.1255 | convolution fusion | flops 4295229440 | bytes 23068672 | tf_op jit(solution)/shard_map/cond/branch_1_fun/dot_general | solution.py:175
  131.3 18.5 %fusion.358 = bf16[128,8,256]{2,0,1:T(8,128)(2,1)} fusion(f32[256,256,8]{1,0,2:T(8,128)} %get-tuple-element.734, f32[8,256]{1,0:T(8,128)S(1)} %get-tuple-element.733, pred[256,256]{0,1:T(8,128)(4,1)S(1)} %iota_compare_fusion.1, bf16[256,8192]{1,0:T(8,128)(2,1)} %fusion.328, bf16[8192,128]{1,0:T(8,128)(2,1)} %get-tuple-element.186), kind=kOutput, calls=%fused_computation.1259 | convolution fusion | flops 672923648 | bytes 8986624 | tf_op jit(solution)/shard_map/cond/branch_1_fun/hgqs,shd->qhgd/dot_general | solution.py:170
  149.8 12.2 %fusion.325 = bf16[256,8192]{1,0:T(8,128)(2,1)S(1)} fusion(bf16[256,1024]{0,1:T(8,128)(2,1)} %bitcast.3186, bf16[1024,8192]{1,0:T(8,128)(2,1)} %get-tuple-element.191, bf16[256,8192]{1,0:T(8,128)(2,1)} %get-tuple-element.184, pred[256]{0:T(512)(128)(4,1)S(1)} %reduce.12), kind=kOutput, calls=%fused_computation.1213 | convolution fusion | flops 4303355904 | bytes 25690368 | tf_op jit(solution)/shard_map/cond/branch_1_fun/dot_general | solution.py:175
  162.0 130.3 %conditional = (bf16[256,8192]{1,0:T(8,128)(2,1)}) conditional(s32[]{:T(128)} %clamp.14, bf16[256,8192]{1,0:T(8,128)(2,1)S(1)} %fusion.325, bf16[256,8192]{1,0:T(8,128)(2,1)S(1)} %fusion.325, bf16[256,8192]{1,0:T(8,128)(2,1)S(1)} %fusion.325, bf16[256,8192]{1,0:T(8,128)(2,1)S(1)} %fusion.325, ...), branch_computations={%region_12.12_spmd, %region_13.13_spmd, %region_14.14_spmd, %regio... | conditional | flops 11534437 | bytes 86247240 | solution.py:262
  173.6 7.7 %collective-permute-start.2 = (bf16[2,16,8192]{2,1,0:T(8,128)(2,1)}, bf16[2,16,8192]{2,1,0:T(8,128)(2,1)}, u32[]{:S(2)}, u32[]{:S(2)}) collective-permute-start(bf16[2,16,8192]{2,1,0:T(8,128)(2,1)} %get-tuple-element.404), channel_id=1, source_target_pairs={{0,6},{2,0},{4,2},{6,4},{1,7},{3,1},{5,3},{7,5}} | collective-permute-start | bytes 1572872 | tf_op jit(solution)/shard_map/cond/branch_1_fun/cond/branch_0_fun/ppermute | solution.py:29
  194.8 33.0 %collective-permute-done.1 = bf16[2,16,8192]{2,1,0:T(8,128)(2,1)} collective-permute-done((bf16[2,16,8192]{2,1,0:T(8,128)(2,1)}, bf16[2,16,8192]{2,1,0:T(8,128)(2,1)}, u32[]{:S(2)}, u32[]{:S(2)}) %collective-permute-start.1) | collective-permute-done | bytes 524320 | tf_op jit(solution)/shard_map/cond/branch_1_fun/cond/branch_0_fun/ppermute | solution.py:29
  252.2 6.6 %collective-permute-done.10 = bf16[16,8192]{1,0:T(8,128)(2,1)S(1)} collective-permute-done((bf16[16,8192]{1,0:T(8,128)(2,1)S(1)}, bf16[16,8192]{1,0:T(8,128)(2,1)S(1)}, u32[]{:S(2)}, u32[]{:S(2)}) %collective-permute-start.10) | collective-permute-done | bytes 262176 | tf_op jit(solution)/shard_map/cond/branch_1_fun/cond/branch_0_fun/ppermute | solution.py:29
  261.2 20.8 %collective-permute-done.12 = bf16[4,16,8192]{2,1,0:T(8,128)(2,1)S(1)} collective-permute-done((bf16[4,16,8192]{2,1,0:T(8,128)(2,1)S(1)}, bf16[4,16,8192]{2,1,0:T(8,128)(2,1)S(1)}, u32[]{:S(2)}, u32[]{:S(2)}) %collective-permute-start.12) | collective-permute-done | bytes 1048608 | tf_op jit(solution)/shard_map/cond/branch_1_fun/cond/branch_0_fun/ppermute | solution.py:34
  294.0 6.1 collective-permute-start.636
  319.5 9.4 %convolution_add_fusion.5 = f32[256,1024]{1,0:T(8,128)S(1)} fusion(f32[256,1024]{1,0:T(8,128)S(1)} %convolution_multiply_fusion.3, bf16[256,8192]{1,0:T(8,128)(2,1)} %copy-done.28, bf16[8192,1024]{1,0:T(8,128)(2,1)} %get-tuple-element.188), kind=kOutput, calls=%fused_computation.1253 | convolution fusion | flops 4295229440 | bytes 23068672 | tf_op jit(solution)/shard_map/cond/branch_1_fun/dot_general | solution.py:175
  353.1 8.0 %collective-permute-done.640 = bf16[64,2048]{1,0:T(8,128)(2,1)S(1)} collective-permute-done((bf16[64,2048]{1,0:T(8,128)(2,1)S(1)}, bf16[64,2048]{1,0:T(8,128)(2,1)S(1)}, u32[]{:S(2)}, u32[]{:S(2)}) %collective-permute-start.640) | collective-permute-done | bytes 262176 | tf_op jit(solution)/shard_map/cond/branch_1_fun/ppermute | solution.py:29
  362.9 5.4 collective-permute-done.643
  369.3 8.5 %collective-permute-done.644 = bf16[2,64,1536]{2,1,0:T(8,128)(2,1)S(1)} collective-permute-done((bf16[2,64,1536]{2,1,0:T(8,128)(2,1)S(1)}, bf16[2,64,1536]{2,1,0:T(8,128)(2,1)S(1)}, u32[]{:S(2)}, u32[]{:S(2)}) %collective-permute-start.644) | collective-permute-done | bytes 393248 | tf_op jit(solution)/shard_map/cond/branch_1_fun/ppermute | solution.py:34
  379.4 11.1 %convolution_bitcast_fusion.3 = bf16[128,8,256]{0,2,1:T(8,128)(2,1)S(1)} fusion(bf16[256,8192,1]{1,0,2:T(8,128)(2,1)S(1)} %bitcast.2921, bf16[8,128,8192]{2,1,0:T(8,128)(2,1)} %bitcast.2910), kind=kOutput, calls=%fused_computation.1257 | convolution fusion | flops 4294967296 | bytes 21495808 | tf_op jit(solution)/shard_map/cond/branch_1_fun/dot_general | solution.py:175
  397.7 13.9 %fusion.390 = f32[256,8192]{1,0:T(8,128)} fusion(bf16[8192,1024]{1,0:T(8,128)(2,1)} %get-tuple-element.188, f32[256,8,64]{2,0,1:T(8,128)} %copy-done.45, f32[256,8,64]{2,0,1:T(8,128)S(1)} %get-tuple-element.719), kind=kOutput, calls=%fused_computation.1300 | convolution fusion | flops 4295229440 | bytes 26214400 | tf_op jit(solution)/shard_map/cond/branch_1_fun/dot_general | solution.py:175
  423.1 9.3 %add_convert_fusion = bf16[256,8192]{1,0:T(8,128)(2,1)} fusion(bf16[4,64,8192]{2,1,0:T(8,128)(2,1)} %copy-done.39, f32[256]{0:T(256)S(1)} %multiply_multiply_fusion, bf16[256,8192]{1,0:T(8,128)(2,1)} %copy-done.38, f32[256,8192]{1,0:T(8,128)} %convolution_add_fusion.2, bf16[8192,16]{0,1:T(8,128)(2,1)S(1)} %get-tuple-element.189, ...), kind=kOutput, calls=%fused_computation.1220 | convolution fusion | flops 96739328 | bytes 22350080 | tf_op jit(solution)/shard_map/cond/branch_1_fun/dot_general | solution.py:175
  432.4 124.5 %conditional.1 = (bf16[256,8192]{1,0:T(8,128)(2,1)}) conditional(s32[]{:T(128)} %clamp.15, bf16[256,8192]{1,0:T(8,128)(2,1)} %add_convert_fusion, bf16[256,8192]{1,0:T(8,128)(2,1)} %add_convert_fusion, bf16[256,8192]{1,0:T(8,128)(2,1)} %add_convert_fusion, bf16[256,8192]{1,0:T(8,128)(2,1)} %add_convert_fusion, ...), branch_computations={%region_24.24_spmd, %region_25.25_spmd, %region_26.26_spmd, %regio... | conditional | flops 11534437 | bytes 97781496 | solution.py:262
  444.4 17.0 %collective-permute-done.73 = bf16[4,16,8192]{2,1,0:T(8,128)(2,1)S(1)} collective-permute-done((bf16[4,16,8192]{2,1,0:T(8,128)(2,1)}, bf16[4,16,8192]{2,1,0:T(8,128)(2,1)S(1)}, u32[]{:S(2)}, u32[]{:S(2)}) %collective-permute-start.73) | collective-permute-done | bytes 1048608 | tf_op jit(solution)/shard_map/cond/branch_1_fun/cond/branch_0_fun/ppermute | solution.py:34
  463.5 9.8 %collective-permute-start.76 = (bf16[16,8192]{1,0:T(8,128)(2,1)S(1)}, bf16[16,8192]{1,0:T(8,128)(2,1)S(1)}, u32[]{:S(2)}, u32[]{:S(2)}) collective-permute-start(bf16[16,8192]{1,0:T(8,128)(2,1)S(1)} %get-tuple-element.460), channel_id=1, source_target_pairs={{0,4},{2,6},{4,0},{6,2},{24,28},{26,30},{28,24},{30,26},{1,5},{3,7... | collective-permute-start | bytes 786440 | tf_op jit(solution)/shard_map/cond/branch_1_fun/cond/branch_0_fun/ppermute | solution.py:29
  476.9 15.4 %collective-permute-done.76 = bf16[16,8192]{1,0:T(8,128)(2,1)S(1)} collective-permute-done((bf16[16,8192]{1,0:T(8,128)(2,1)S(1)}, bf16[16,8192]{1,0:T(8,128)(2,1)S(1)}, u32[]{:S(2)}, u32[]{:S(2)}) %collective-permute-start.76) | collective-permute-done | bytes 262176 | tf_op jit(solution)/shard_map/cond/branch_1_fun/cond/branch_0_fun/ppermute | solution.py:29
  493.8 10.8 %collective-permute-done.78 = bf16[16,8192]{1,0:T(8,128)(2,1)S(1)} collective-permute-done((bf16[16,8192]{1,0:T(8,128)(2,1)S(1)}, bf16[16,8192]{1,0:T(8,128)(2,1)S(1)}, u32[]{:S(2)}, u32[]{:S(2)}) %collective-permute-start.78) | collective-permute-done | bytes 262176 | tf_op jit(solution)/shard_map/cond/branch_1_fun/cond/branch_0_fun/ppermute | solution.py:34
  511.0 5.7 collective-permute-start.85
  519.5 6.1 collective-permute-done.83
  525.6 18.2 %collective-permute-done.84 = bf16[2,16,8192]{2,1,0:T(8,128)(2,1)S(1)} collective-permute-done((bf16[2,16,8192]{2,1,0:T(8,128)(2,1)S(1)}, bf16[2,16,8192]{2,1,0:T(8,128)(2,1)S(1)}, u32[]{:S(2)}, u32[]{:S(2)}) %collective-permute-start.84) | collective-permute-done | bytes 524320 | tf_op jit(solution)/shard_map/cond/branch_1_fun/cond/branch_0_fun/ppermute | solution.py:29
  560.8 8.5 %fusion.694 = bf16[256,1024]{0,1:T(8,128)(2,1)S(1)} fusion(bf16[256,8192]{1,0:T(8,128)(2,1)S(1)} %bitcast_select_fusion.2, bf16[1024,8192]{1,0:T(8,128)(2,1)} %get-tuple-element.191), kind=kOutput, calls=%fused_computation.1689 | convolution fusion | flops 4294967296 | bytes 21495808 | tf_op jit(solution)/shard_map/cond/branch_1_fun/transpose(jvp())/reshape | solution.py:171
  572.4 6.3 %collective-permute-start.646 = (f32[256,16]{0,1:T(8,128)S(1)}, f32[256,16]{0,1:T(8,128)S(1)}, u32[]{:S(2)}, u32[]{:S(2)}) collective-permute-start(f32[256,16]{0,1:T(8,128)S(1)} %convolution_multiply_fusion.6), channel_id=1, source_target_pairs={{0,2},{2,0},{4,6},{6,4},{1,3},{3,1},{5,7},{7,5},{8,10},{10,8},{12,... | collective-permute-start | bytes 49160 | tf_op jit(solution)/shard_map/cond/branch_1_fun/ppermute | solution.py:123
  (357 shorter events, 263.6 us)
Async XLA Ops:
  3.3 39.5 %collective-permute-start.660 = (bf16[64,1536]{1,0:T(8,128)(2,1)}, bf16[64,1536]{1,0:T(8,128)(2,1)S(1)}, u32[]{:S(2)}, u32[]{:S(2)}) collective-permute-start(bf16[64,1536]{1,0:T(8,128)(2,1)} %get-tuple-element.789), channel_id=1, source_target_pairs={{0,2},{2,4},{4,6},{6,0},{8,10},{10,12},{12,14},{14,8},{16,18},{18,... | collective-permute-start | bytes 589832 | tf_op jit(solution)/shard_map/ppermute | solution.py:29
  6.3 37.1 %collective-permute-start.661 = (bf16[64,1536]{1,0:T(8,128)(2,1)}, bf16[64,1536]{1,0:T(8,128)(2,1)S(1)}, u32[]{:S(2)}, u32[]{:S(2)}) collective-permute-start(bf16[64,1536]{1,0:T(8,128)(2,1)} %get-tuple-element.789), channel_id=1, source_target_pairs={{0,4},{2,6},{4,0},{6,2},{8,12},{10,14},{12,8},{14,10},{16,20},{18,... | collective-permute-start | bytes 589832 | tf_op jit(solution)/shard_map/ppermute | solution.py:29
  8.9 35.2 %collective-permute-start.662 = (bf16[64,1536]{1,0:T(8,128)(2,1)}, bf16[64,1536]{1,0:T(8,128)(2,1)S(1)}, u32[]{:S(2)}, u32[]{:S(2)}) collective-permute-start(bf16[64,1536]{1,0:T(8,128)(2,1)} %get-tuple-element.789), channel_id=1, source_target_pairs={{0,6},{2,0},{4,2},{6,4},{8,14},{10,8},{12,10},{14,12},{16,22},{18,... | collective-permute-start | bytes 589832 | tf_op jit(solution)/shard_map/ppermute | solution.py:29
  46.4 19.6 %collective-permute-start.664 = (bf16[64,2048]{1,0:T(8,128)(2,1)S(1)}, bf16[64,2048]{1,0:T(8,128)(2,1)S(1)}, u32[]{:S(2)}, u32[]{:S(2)}) collective-permute-start(bf16[64,2048]{1,0:T(8,128)(2,1)S(1)} %slice.804), channel_id=1, source_target_pairs={{0,4},{2,6},{4,0},{6,2},{8,12},{10,14},{12,8},{14,10},{16,20},{18,... | collective-permute-start | bytes 786440 | tf_op jit(solution)/shard_map/ppermute | solution.py:29
  50.3 21.9 %collective-permute-start.666 = (bf16[4,64,1536]{2,1,0:T(8,128)(2,1)}, bf16[4,64,1536]{2,1,0:T(8,128)(2,1)S(1)}, u32[]{:S(2)}, u32[]{:S(2)}) collective-permute-start(bf16[4,64,1536]{2,1,0:T(8,128)(2,1)} %bitcast_dynamic-update-slice_fusion.316), channel_id=1, source_target_pairs={{0,8},{2,10},{4,12},{6,14},{8,0},{10,2},{12,4},{14,6},{16,24},{18,... | collective-permute-start | bytes 2359304 | tf_op jit(solution)/shard_map/ppermute | solution.py:34
  51.7 18.8 %collective-permute-start.667 = (bf16[4,64,1536]{2,1,0:T(8,128)(2,1)}, bf16[4,64,1536]{2,1,0:T(8,128)(2,1)S(1)}, u32[]{:S(2)}, u32[]{:S(2)}) collective-permute-start(bf16[4,64,1536]{2,1,0:T(8,128)(2,1)} %bitcast_dynamic-update-slice_fusion.316), channel_id=1, source_target_pairs={{0,16},{2,18},{4,20},{6,22},{8,24},{10,26},{12,28},{14,30},{16,0},... | collective-permute-start | bytes 2359304 | tf_op jit(solution)/shard_map/ppermute | solution.py:34
  163.5 24.8 %collective-permute-start.3 = (bf16[4,16,8192]{2,1,0:T(8,128)(2,1)}, bf16[4,16,8192]{2,1,0:T(8,128)(2,1)}, u32[]{:S(2)}, u32[]{:S(2)}) collective-permute-start(bf16[4,16,8192]{2,1,0:T(8,128)(2,1)} %get-tuple-element.402), channel_id=1, source_target_pairs={{0,8},{2,10},{4,12},{6,14},{1,9},{3,11},{5,13},{7,15}} | collective-permute-start | bytes 3145736 | tf_op jit(solution)/shard_map/cond/branch_1_fun/cond/branch_0_fun/ppermute | solution.py:34
  167.3 23.2 %collective-permute-start.4 = (bf16[4,16,8192]{2,1,0:T(8,128)(2,1)}, bf16[4,16,8192]{2,1,0:T(8,128)(2,1)}, u32[]{:S(2)}, u32[]{:S(2)}) collective-permute-start(bf16[4,16,8192]{2,1,0:T(8,128)(2,1)} %get-tuple-element.401), channel_id=1, source_target_pairs={{0,16},{2,18},{4,20},{6,22},{1,17},{3,19},{5,21},{7,23}} | collective-permute-start | bytes 3145736 | tf_op jit(solution)/shard_map/cond/branch_1_fun/cond/branch_0_fun/ppermute | solution.py:34
  173.6 20.5 %collective-permute-start.2 = (bf16[2,16,8192]{2,1,0:T(8,128)(2,1)}, bf16[2,16,8192]{2,1,0:T(8,128)(2,1)}, u32[]{:S(2)}, u32[]{:S(2)}) collective-permute-start(bf16[2,16,8192]{2,1,0:T(8,128)(2,1)} %get-tuple-element.404), channel_id=1, source_target_pairs={{0,6},{2,0},{4,2},{6,4},{1,7},{3,1},{5,3},{7,5}} | collective-permute-start | bytes 1572872 | tf_op jit(solution)/shard_map/cond/branch_1_fun/cond/branch_0_fun/ppermute | solution.py:29
  181.3 46.5 %collective-permute-start.1 = (bf16[2,16,8192]{2,1,0:T(8,128)(2,1)}, bf16[2,16,8192]{2,1,0:T(8,128)(2,1)}, u32[]{:S(2)}, u32[]{:S(2)}) collective-permute-start(bf16[2,16,8192]{2,1,0:T(8,128)(2,1)} %get-tuple-element.405), channel_id=1, source_target_pairs={{0,4},{2,6},{4,0},{6,2},{1,5},{3,7},{5,1},{7,3}} | collective-permute-start | bytes 1572872 | tf_op jit(solution)/shard_map/cond/branch_1_fun/cond/branch_0_fun/ppermute | solution.py:29
  185.0 42.8 %collective-permute-start = (bf16[2,16,8192]{2,1,0:T(8,128)(2,1)}, bf16[2,16,8192]{2,1,0:T(8,128)(2,1)}, u32[]{:S(2)}, u32[]{:S(2)}) collective-permute-start(bf16[2,16,8192]{2,1,0:T(8,128)(2,1)} %get-tuple-element.403), channel_id=1, source_target_pairs={{0,2},{2,4},{4,6},{6,0},{1,3},{3,5},{5,7},{7,1}} | collective-permute-start | bytes 1572872 | tf_op jit(solution)/shard_map/cond/branch_1_fun/cond/branch_0_fun/ppermute | solution.py:29
  191.9 37.6 %collective-permute-start.7 = (bf16[16,8192]{1,0:T(8,128)(2,1)S(1)}, bf16[16,8192]{1,0:T(8,128)(2,1)S(1)}, u32[]{:S(2)}, u32[]{:S(2)}) collective-permute-start(bf16[16,8192]{1,0:T(8,128)(2,1)S(1)} %get-tuple-element.407), channel_id=1, source_target_pairs={{8,14},{10,8},{12,10},{14,12},{16,22},{18,16},{20,18},{22,20},{9,1... | collective-permute-start | bytes 786440 | tf_op jit(solution)/shard_map/cond/branch_1_fun/cond/branch_0_fun/ppermute | solution.py:29
  192.6 37.0 %collective-permute-start.6 = (bf16[16,8192]{1,0:T(8,128)(2,1)S(1)}, bf16[16,8192]{1,0:T(8,128)(2,1)S(1)}, u32[]{:S(2)}, u32[]{:S(2)}) collective-permute-start(bf16[16,8192]{1,0:T(8,128)(2,1)S(1)} %get-tuple-element.408), channel_id=1, source_target_pairs={{8,12},{10,14},{12,8},{14,10},{16,20},{18,22},{20,16},{22,18},{9,1... | collective-permute-start | bytes 786440 | tf_op jit(solution)/shard_map/cond/branch_1_fun/cond/branch_0_fun/ppermute | solution.py:29
  194.1 35.5 %collective-permute-start.5 = (bf16[16,8192]{1,0:T(8,128)(2,1)S(1)}, bf16[16,8192]{1,0:T(8,128)(2,1)S(1)}, u32[]{:S(2)}, u32[]{:S(2)}) collective-permute-start(bf16[16,8192]{1,0:T(8,128)(2,1)S(1)} %get-tuple-element.406), channel_id=1, source_target_pairs={{8,10},{10,12},{12,14},{14,8},{16,18},{18,20},{20,22},{22,16},{9,1... | collective-permute-start | bytes 786440 | tf_op jit(solution)/shard_map/cond/branch_1_fun/cond/branch_0_fun/ppermute | solution.py:29
  239.2 19.6 %collective-permute-start.10 = (bf16[16,8192]{1,0:T(8,128)(2,1)S(1)}, bf16[16,8192]{1,0:T(8,128)(2,1)S(1)}, u32[]{:S(2)}, u32[]{:S(2)}) collective-permute-start(bf16[16,8192]{1,0:T(8,128)(2,1)S(1)} %get-tuple-element.234), channel_id=1, source_target_pairs={{0,4},{2,6},{4,0},{6,2},{24,28},{26,30},{28,24},{30,26},{1,5},{3,7... | collective-permute-start | bytes 786440 | tf_op jit(solution)/shard_map/cond/branch_1_fun/cond/branch_0_fun/ppermute | solution.py:29
  259.6 22.4 %collective-permute-start.12 = (bf16[4,16,8192]{2,1,0:T(8,128)(2,1)S(1)}, bf16[4,16,8192]{2,1,0:T(8,128)(2,1)S(1)}, u32[]{:S(2)}, u32[]{:S(2)}) collective-permute-start(bf16[4,16,8192]{2,1,0:T(8,128)(2,1)S(1)} %bitcast_dynamic-update-slice_fusion.12), channel_id=1, source_target_pairs={{0,8},{2,10},{4,12},{6,14},{1,9},{3,11},{5,13},{7,15}} | collective-permute-start | bytes 3145736 | tf_op jit(solution)/shard_map/cond/branch_1_fun/cond/branch_0_fun/ppermute | solution.py:34
  294.0 42.7 %collective-permute-start.636 = (bf16[64,1536]{1,0:T(8,128)(2,1)}, bf16[64,1536]{1,0:T(8,128)(2,1)}, u32[]{:S(2)}, u32[]{:S(2)}) collective-permute-start(bf16[64,1536]{1,0:T(8,128)(2,1)} %get-tuple-element.378), channel_id=1, source_target_pairs={{0,2},{2,4},{4,6},{6,0},{8,10},{10,12},{12,14},{14,8},{16,18},{18,... | collective-permute-start | bytes 589832 | tf_op jit(solution)/shard_map/cond/branch_1_fun/ppermute | solution.py:29
  300.2 38.5 %collective-permute-start.637 = (bf16[64,1536]{1,0:T(8,128)(2,1)}, bf16[64,1536]{1,0:T(8,128)(2,1)}, u32[]{:S(2)}, u32[]{:S(2)}) collective-permute-start(bf16[64,1536]{1,0:T(8,128)(2,1)} %get-tuple-element.378), channel_id=1, source_target_pairs={{0,4},{2,6},{4,0},{6,2},{8,12},{10,14},{12,8},{14,10},{16,20},{18,... | collective-permute-start | bytes 589832 | tf_op jit(solution)/shard_map/cond/branch_1_fun/ppermute | solution.py:29
  302.7 37.6 %collective-permute-start.638 = (bf16[64,1536]{1,0:T(8,128)(2,1)}, bf16[64,1536]{1,0:T(8,128)(2,1)}, u32[]{:S(2)}, u32[]{:S(2)}) collective-permute-start(bf16[64,1536]{1,0:T(8,128)(2,1)} %get-tuple-element.378), channel_id=1, source_target_pairs={{0,6},{2,0},{4,2},{6,4},{8,14},{10,8},{12,10},{14,12},{16,22},{18,... | collective-permute-start | bytes 589832 | tf_op jit(solution)/shard_map/cond/branch_1_fun/ppermute | solution.py:29
  346.8 21.9 %collective-permute-start.642 = (bf16[4,64,1536]{2,1,0:T(8,128)(2,1)}, bf16[4,64,1536]{2,1,0:T(8,128)(2,1)S(1)}, u32[]{:S(2)}, u32[]{:S(2)}) collective-permute-start(bf16[4,64,1536]{2,1,0:T(8,128)(2,1)} %bitcast_dynamic-update-slice_fusion.300), channel_id=1, source_target_pairs={{0,8},{2,10},{4,12},{6,14},{8,0},{10,2},{12,4},{14,6},{16,24},{18,... | collective-permute-start | bytes 2359304 | tf_op jit(solution)/shard_map/cond/branch_1_fun/ppermute | solution.py:34
  435.6 25.7 %collective-permute-start.73 = (bf16[4,16,8192]{2,1,0:T(8,128)(2,1)}, bf16[4,16,8192]{2,1,0:T(8,128)(2,1)S(1)}, u32[]{:S(2)}, u32[]{:S(2)}) collective-permute-start(bf16[4,16,8192]{2,1,0:T(8,128)(2,1)} %get-tuple-element.454), channel_id=1, source_target_pairs={{8,0},{10,2},{12,4},{14,6},{9,1},{11,3},{13,5},{15,7}} | collective-permute-start | bytes 3145736 | tf_op jit(solution)/shard_map/cond/branch_1_fun/cond/branch_0_fun/ppermute | solution.py:34
  436.9 24.4 %collective-permute-start.74 = (bf16[4,16,8192]{2,1,0:T(8,128)(2,1)}, bf16[4,16,8192]{2,1,0:T(8,128)(2,1)}, u32[]{:S(2)}, u32[]{:S(2)}) collective-permute-start(bf16[4,16,8192]{2,1,0:T(8,128)(2,1)} %get-tuple-element.453), channel_id=1, source_target_pairs={{8,24},{10,26},{12,28},{14,30},{9,25},{11,27},{13,29},{15,31}} | collective-permute-start | bytes 3145736 | tf_op jit(solution)/shard_map/cond/branch_1_fun/cond/branch_0_fun/ppermute | solution.py:34
  440.0 33.3 %collective-permute-start.72 = (bf16[2,16,8192]{2,1,0:T(8,128)(2,1)}, bf16[2,16,8192]{2,1,0:T(8,128)(2,1)}, u32[]{:S(2)}, u32[]{:S(2)}) collective-permute-start(bf16[2,16,8192]{2,1,0:T(8,128)(2,1)} %get-tuple-element.456), channel_id=1, source_target_pairs={{8,14},{10,8},{12,10},{14,12},{9,15},{11,9},{13,11},{15,13}} | collective-permute-start | bytes 1572872 | tf_op jit(solution)/shard_map/cond/branch_1_fun/cond/branch_0_fun/ppermute | solution.py:29
  441.4 33.8 %collective-permute-start.71 = (bf16[2,16,8192]{2,1,0:T(8,128)(2,1)}, bf16[2,16,8192]{2,1,0:T(8,128)(2,1)}, u32[]{:S(2)}, u32[]{:S(2)}) collective-permute-start(bf16[2,16,8192]{2,1,0:T(8,128)(2,1)} %get-tuple-element.457), channel_id=1, source_target_pairs={{8,12},{10,14},{12,8},{14,10},{9,13},{11,15},{13,9},{15,11}} | collective-permute-start | bytes 1572872 | tf_op jit(solution)/shard_map/cond/branch_1_fun/cond/branch_0_fun/ppermute | solution.py:29
  442.9 32.3 %collective-permute-start.70 = (bf16[2,16,8192]{2,1,0:T(8,128)(2,1)}, bf16[2,16,8192]{2,1,0:T(8,128)(2,1)}, u32[]{:S(2)}, u32[]{:S(2)}) collective-permute-start(bf16[2,16,8192]{2,1,0:T(8,128)(2,1)} %get-tuple-element.455), channel_id=1, source_target_pairs={{8,10},{10,12},{12,14},{14,8},{9,11},{11,13},{13,15},{15,9}} | collective-permute-start | bytes 1572872 | tf_op jit(solution)/shard_map/cond/branch_1_fun/cond/branch_0_fun/ppermute | solution.py:29
  463.5 28.8 %collective-permute-start.76 = (bf16[16,8192]{1,0:T(8,128)(2,1)S(1)}, bf16[16,8192]{1,0:T(8,128)(2,1)S(1)}, u32[]{:S(2)}, u32[]{:S(2)}) collective-permute-start(bf16[16,8192]{1,0:T(8,128)(2,1)S(1)} %get-tuple-element.460), channel_id=1, source_target_pairs={{0,4},{2,6},{4,0},{6,2},{24,28},{26,30},{28,24},{30,26},{1,5},{3,7... | collective-permute-start | bytes 786440 | tf_op jit(solution)/shard_map/cond/branch_1_fun/cond/branch_0_fun/ppermute | solution.py:29
  473.3 19.0 %collective-permute-start.75 = (bf16[16,8192]{1,0:T(8,128)(2,1)S(1)}, bf16[16,8192]{1,0:T(8,128)(2,1)S(1)}, u32[]{:S(2)}, u32[]{:S(2)}) collective-permute-start(bf16[16,8192]{1,0:T(8,128)(2,1)S(1)} %get-tuple-element.458), channel_id=1, source_target_pairs={{0,2},{2,4},{4,6},{6,0},{24,26},{26,28},{28,30},{30,24},{1,3},{3,5... | collective-permute-start | bytes 786440 | tf_op jit(solution)/shard_map/cond/branch_1_fun/cond/branch_0_fun/ppermute | solution.py:29
  506.9 18.7 %collective-permute-start.83 = (bf16[2,16,8192]{2,1,0:T(8,128)(2,1)S(1)}, bf16[2,16,8192]{2,1,0:T(8,128)(2,1)S(1)}, u32[]{:S(2)}, u32[]{:S(2)}) collective-permute-start(bf16[2,16,8192]{2,1,0:T(8,128)(2,1)S(1)} %pad_maximum_fusion.13), channel_id=1, source_target_pairs={{0,2},{2,4},{4,6},{6,0},{1,3},{3,5},{5,7},{7,1}} | collective-permute-start | bytes 1572872 | tf_op jit(solution)/shard_map/cond/branch_1_fun/cond/branch_0_fun/ppermute | solution.py:29
  508.9 35.0 %collective-permute-start.84 = (bf16[2,16,8192]{2,1,0:T(8,128)(2,1)S(1)}, bf16[2,16,8192]{2,1,0:T(8,128)(2,1)S(1)}, u32[]{:S(2)}, u32[]{:S(2)}) collective-permute-start(bf16[2,16,8192]{2,1,0:T(8,128)(2,1)S(1)} %pad_maximum_fusion.13), channel_id=1, source_target_pairs={{0,4},{2,6},{4,0},{6,2},{1,5},{3,7},{5,1},{7,3}} | collective-permute-start | bytes 1572872 | tf_op jit(solution)/shard_map/cond/branch_1_fun/cond/branch_0_fun/ppermute | solution.py:29
  511.0 32.8 %collective-permute-start.85 = (bf16[2,16,8192]{2,1,0:T(8,128)(2,1)S(1)}, bf16[2,16,8192]{2,1,0:T(8,128)(2,1)S(1)}, u32[]{:S(2)}, u32[]{:S(2)}) collective-permute-start(bf16[2,16,8192]{2,1,0:T(8,128)(2,1)S(1)} %pad_maximum_fusion.13), channel_id=1, source_target_pairs={{0,6},{2,0},{4,2},{6,4},{1,7},{3,1},{5,3},{7,5}} | collective-permute-start | bytes 1572872 | tf_op jit(solution)/shard_map/cond/branch_1_fun/cond/branch_0_fun/ppermute | solution.py:29
  516.9 29.9 %collective-permute-start.86 = (bf16[4,16,8192]{2,1,0:T(8,128)(2,1)S(1)}, bf16[4,16,8192]{2,1,0:T(8,128)(2,1)S(1)}, u32[]{:S(2)}, u32[]{:S(2)}) collective-permute-start(bf16[4,16,8192]{2,1,0:T(8,128)(2,1)S(1)} %bitcast_dynamic-update-slice_fusion.60), channel_id=1, source_target_pairs={{16,0},{18,2},{20,4},{22,6},{17,1},{19,3},{21,5},{23,7}} | collective-permute-start | bytes 3145736 | tf_op jit(solution)/shard_map/cond/branch_1_fun/cond/branch_0_fun/ppermute | solution.py:34
  518.2 31.9 %collective-permute-start.82 = (bf16[4,16,8192]{2,1,0:T(8,128)(2,1)S(1)}, bf16[4,16,8192]{2,1,0:T(8,128)(2,1)S(1)}, u32[]{:S(2)}, u32[]{:S(2)}) collective-permute-start(bf16[4,16,8192]{2,1,0:T(8,128)(2,1)S(1)} %bitcast_dynamic-update-slice_fusion.60), channel_id=1, source_target_pairs={{8,0},{10,2},{12,4},{14,6},{9,1},{11,3},{13,5},{15,7}} | collective-permute-start | bytes 3145736 | tf_op jit(solution)/shard_map/cond/branch_1_fun/cond/branch_0_fun/ppermute | solution.py:34
  (80 other events, 1016.7 us)
